TPU v7x, 128 devices: a whole 4x4x4 slice. The times are simulated.
128 devices in a mesh: gx: 4 (over x_lo, core), gy: 4 (over y), gz: 8 (over x_hi, z).
Axes of the slice: x: 4 (x_hi: 2, x_lo: 2; x = x_hi * 2 + x_lo), y: 4, z: 4, core: 2. Of those that a mesh axis runs over, the one named last changes fastest.
Arguments:
- positions: float32 [3, 2048, 128], P(None, ('gx', 'gy', 'gz')), may hold values from -6 to 6
- velocities: float32 [3, 2048, 128], P(None, ('gx', 'gy', 'gz')), may hold values from -6 to 6
- weights: float32 [2048, 128], P(('gx', 'gy', 'gz')), may hold values from 0.5 to 2
- counts: int32 [2048], P(('gx', 'gy', 'gz')), may hold values from 32 to 128
- link_offset: int32 [2048, 3], P(('gx', 'gy', 'gz')), may hold values from -16 to 16
- link_mask: int32 [2048, 3], P(('gx', 'gy', 'gz')), may hold values 0 or 1
- bin_box: int32 [2048, 1], P(('gx', 'gy', 'gz')), may hold values from 0 to 15; in each aligned block of 16 rows (0 to 15, 16 to 31, ...) at most 2 rows name the same one
- bin_cell: int32 [2048], P(('gx', 'gy', 'gz')), may hold values from 0 to 4095
- fluid: float32 [3, 16, 32, 1024], P(None, 'gx', 'gy', 'gz'), may hold values from -6 to 6
Outputs:
- positions_out: float32 [3, 2048, 128], P(None, ('gx', 'gy', 'gz'))
- velocities_out: float32 [3, 2048, 128], P(None, ('gx', 'gy', 'gz'))
- fluid_out: float32 [3, 16, 32, 1024], P(None, 'gx', 'gy', 'gz')
Inputs may be any that keep to these rules, and one draw needn't show every extreme that they name: `bin_box`: the bins of one device name one value at most 2 times; the cell lies in the box at the bin owner's index of gz. `bin_cell`: index of the cell inside its box, first dimension slowest. Slots 0 to counts - 1 of a bin are occupied.
All inputs are finite; a program needn't handle non-finite values. No bound on the sum of `link_mask` on one device may be relied on, other than what follows from the above.
Results may differ from a plain program's by a relative error of at most 0.0001.
Values sent between devices are 32-bit elements; how exact they have to be, the bound alone decides.
A program may use at most 128 MiB of HBM per device.

v0:
```python
import jax
import jax.numpy as jnp
from jax import lax
from jax.sharding import PartitionSpec as P

SUBSTEPS = 2
step_sub = 0.1
stiffness = 0.05
damping = 0.05
drag_rate = 1.0
coupling = 0.004
viscosity = 0.12
highest = lax.Precision.HIGHEST


def padded_2(cells, sides, width):
    for axis, dim in sides:
        count = lax.axis_size(axis)
        ends = count - 1
        head = lax.slice_in_dim(cells, 0, width, axis=dim)
        tail = lax.slice_in_dim(cells, cells.shape[dim] - width, cells.shape[dim], axis=dim)
        cells = jnp.concatenate(
            [
                lax.ppermute(tail, axis, [(i, (i + 1) % count) for i in range(ends)]),
                cells,
                lax.ppermute(head, axis, [((i + 1) % count, i) for i in range(ends)]),
            ],
            axis=dim,
        )
    return cells


def contact(own_pos, own_vel, near_pos, near_vel, near_weight):
    distance = jnp.zeros(
        near_weight.shape[:2] + (own_pos.shape[2], near_weight.shape[2]), jnp.float32
    )
    for component in range(3):
        offset = own_pos[component][:, None, :, None] - near_pos[component][:, :, None, :]
        distance = distance + offset * offset
    kernel = near_weight[:, :, None, :] * jnp.exp(-0.5 * distance)
    weight_sum = jnp.sum(kernel, axis=(1, 3))
    pull_pos = jnp.einsum("bqij,cbqj->cbi", kernel, near_pos, precision=highest)
    pull_vel = jnp.einsum("bqij,cbqj->cbi", kernel, near_vel, precision=highest)
    return stiffness * (own_pos * weight_sum[None] - pull_pos) - damping * (
        own_vel * weight_sum[None] - pull_vel
    )


def advance(
    widened, state_pos, state_vel, carried, occupied, fluid_seen, neighbour, link_weight, block_bins
):
    bin_count = state_pos.shape[1]

    def one_block(block_id, running):
        nearby = widened[:, neighbour]
        near_pos = jnp.concatenate([state_pos[:, :, None], nearby[0:3]], 2)
        near_vel = jnp.concatenate([state_vel[:, :, None], nearby[3:6]], 2)
        near_weight = jnp.concatenate([carried[:, None], nearby[6] * link_weight[:, :, None]], 1)
        contact_force = contact(state_pos, state_vel, near_pos, near_vel, near_weight)
        drag_force = drag_rate * (fluid_seen[:, :, None] - state_vel)
        moved_vel = state_vel + step_sub * occupied[None] * (contact_force + drag_force)
        moved_pos = state_pos + step_sub * occupied[None] * moved_vel
        pulled_block = jnp.sum(carried[None] * drag_force, axis=2)
        return (moved_pos, moved_vel, pulled_block)

    start_state = (
        jnp.zeros_like(state_pos),
        jnp.zeros_like(state_vel),
        jnp.zeros((3, bin_count), jnp.float32),
    )
    return lax.fori_loop(0, bin_count // block_bins, one_block, start_state)


def stencil(padded):
    centre = padded[:, 1:-1, 1:-1, 1:-1]
    beside_all = padded[:, 2:, 1:-1, 1:-1] + padded[:, :-2, 1:-1, 1:-1]
    beside_all = beside_all + padded[:, 1:-1, 2:, 1:-1] + padded[:, 1:-1, :-2, 1:-1]
    beside_all = beside_all + padded[:, 1:-1, 1:-1, 2:] + padded[:, 1:-1, 1:-1, :-2]
    return beside_all - 6.0 * centre


def local(positions, velocities, weights, counts, link_offset, link_mask, bin_box, bin_cell, fluid):
    bin_count = positions.shape[1]
    slot_count = positions.shape[2]
    cell_count = fluid.shape[1] * fluid.shape[2] * fluid.shape[3]
    flat_fluid = fluid.reshape(3, cell_count)
    occupied = (
        lax.broadcasted_iota(jnp.int32, (bin_count, slot_count), 1) < counts[:, None]
    ).astype(jnp.float32)
    carried = weights * occupied
    target = bin_box[:, 0]
    box_piece = lax.all_gather(flat_fluid[None], ("gx", "gy"), axis=0, tiled=True)
    first_box = jnp.int32(0)
    local_box = jnp.clip(target, 0, box_piece.shape[0] - 1)
    inside = (target >= first_box) & (target < first_box + box_piece.shape[0])
    picked = box_piece[local_box, :, bin_cell]
    fluid_seen = jnp.where(inside[:, None], picked, 0.0).T
    neighbour = lax.broadcasted_iota(jnp.int32, (bin_count, 1), 0) + link_offset + bin_count
    link_weight = link_mask.astype(jnp.float32)
    block_bins = 16
    state_pos = positions
    state_vel = velocities
    pulled_total = jnp.zeros((3, bin_count), jnp.float32)
    for substep in range(SUBSTEPS):
        packed = jnp.concatenate([state_pos, state_vel, carried[None]], 0)
        widened = padded_2(packed, ((("gx", "gy", "gz"), 1),), bin_count)
        state_pos, state_vel, pulled = advance(
            widened,
            state_pos,
            state_vel,
            carried,
            occupied,
            fluid_seen,
            neighbour,
            link_weight,
            block_bins,
        )
        pulled_total = pulled_total + pulled
    pushed_all = -coupling * pulled_total.T
    first_box = jnp.int32(0)
    local_box = jnp.clip(target, 0, 1 * lax.axis_size(("gx", "gy")) - 1)
    inside = (target >= first_box) & (target < first_box + 1 * lax.axis_size(("gx", "gy")))
    pushed = jnp.where(inside[:, None], pushed_all, 0.0)
    source = lax.psum_scatter(
        jnp.zeros((1 * lax.axis_size(("gx", "gy")), 3, cell_count), jnp.float32)
        .at[local_box, :, bin_cell]
        .add(pushed),
        ("gx", "gy"),
        scatter_dimension=0,
        tiled=True,
    ).reshape(fluid.shape)

    def fluid_rate(velocity_field):
        padded = padded_2(velocity_field, (("gx", 1), ("gy", 2), ("gz", 3)), 1)
        return viscosity * stencil(padded) + source

    first_rate = fluid_rate(fluid)
    middle = fluid + first_rate
    second_rate = fluid_rate(middle)
    fluid_out = fluid + 0.5 * (first_rate + second_rate)
    return (state_pos, state_vel, fluid_out)


def solution(mesh):
    in_specs = (
        P(None, ("gx", "gy", "gz"), None),
        P(None, ("gx", "gy", "gz"), None),
        P(("gx", "gy", "gz"), None),
        P(("gx", "gy", "gz")),
        P(("gx", "gy", "gz"), None),
        P(("gx", "gy", "gz"), None),
        P(("gx", "gy", "gz"), None),
        P(("gx", "gy", "gz")),
        P(None, "gx", "gy", "gz"),
    )
    out_specs = (
        P(None, ("gx", "gy", "gz"), None),
        P(None, ("gx", "gy", "gz"), None),
        P(None, "gx", "gy", "gz"),
    )
    return jax.shard_map(local, mesh=mesh, in_specs=in_specs, out_specs=out_specs, check_vma=False)
```

profile of v0, /device:TPU:6, one launch (start us, length us, event | category | flops | bytes accessed | tf_op | source)
XLA Modules:
  0.0 504.4 jit_solution(973373740408308659)
XLA Ops:
  7.2 0.8 copy.128
  8.0 0.8 copy.127
  8.7 0.8 fusion.94
  9.5 6.8 %collective-permute-start.1 = (f32[7,16,128]{2,0,1:T(8,128)S(1)}, f32[7,16,128]{2,0,1:T(8,128)S(1)}, u32[]{:S(2)}, u32[]{:S(2)}) collective-permute-start(f32[7,16,128]{2,0,1:T(8,128)S(1)} %pad_maximum_fusion.5), channel_id=1, source_target_pairs={{1,0},{2,1},{3,2},{4,3},{5,4},{6,5},{7,6},{8,7},{9,8},{10,9},{11,1... | collective-permute-start | bytes 172040 | tf_op jit(solution)/shard_map/ppermute | solution.py:26
  16.3 1.9 collective-permute-start
  18.3 0.7 fusion.115
  19.0 1.9 collective-permute-start.5
  20.9 3.6 collective-permute-start.4
  24.6 0.8 broadcast_in_dim_reshape.3
  25.4 0.7 slice_bitcast_fusion.2
  26.1 34.2 %all_gather.3 = f32[16,3,4096]{2,1,0:T(4,128)S(1)} all-gather(f32[1,3,4096]{2,1,0:T(4,128)S(1)} %broadcast_in_dim_reshape.3), channel_id=1, replica_groups=mesh['gx'=4,'gy'=4,'gz'=8] {'gx','gy'}, dimensions={0}, use_global_device_ids=true | all-gather | bytes 835584 | tf_op jit(solution)/shard_map/all_gather | solution.py:92
  60.3 15.6 %copy.101 = f32[16,3,4096]{1,2,0:T(8,128)} copy(f32[16,3,4096]{2,1,0:T(4,128)S(1)} %all_gather.3) | data formatting | bytes 1572864 | tf_op jit(solution)/shard_map/all_gather | solution.py:92
  76.0 0.1 reshape.48
  76.1 1.3 gather_fusion.1
  77.6 0.6 gather_fusion
  78.5 2.3 fusion.2
  80.8 5.6 %fusion.49 = f32[3,16,128]{2,0,1:T(4,128)S(1)} fusion(f32[16,4,128]{2,1,0:T(4,128)S(1)} %bitcast.141, f32[16,128]{1,0:T(8,128)S(1)} %get-tuple-element.117, f32[16,4,128]{2,1,0:T(4,128)S(1)} %bitcast.144, f32[16,128]{1,0:T(8,128)S(1)} %get-tuple-element.116, f32[16,4,128]{2,1,0:T(4,128)S(1)} %bitcast.138, f32[16,128]{1,0:T(8,128)S(1)} %get-tuple-element.115, ...), kind=kOutput, calls=%fused_computation.55 | convolution fusion | flops 48277504 | bytes 311296 | tf_op jit(solution)/shard_map/while/body/eval_jaxpr/bqij,cbqj->cbi/dot_general | solution.py:42
  86.4 5.9 %multiply_reduce_fusion = (f32[3,16]{0,1:T(8,128)S(1)}, f32[3,16]{0,1:T(8,128)S(1)}, f32[3,16,128]{2,0,1:T(4,128)S(1)}, f32[3,16,128]{2,0,1:T(4,128)S(1)}) fusion(f32[16,128]{1,0:T(8,128)S(1)} %get-tuple-element.121, f32[3,16]{0,1:T(8,128)S(1)} %select_bitcast_fusion.1, f32[3,16,128]{2,1,0:T(8,128)S(1)} %copy-done.2, ...), kind=kOutput, calls=%fused_computation.141 | convolution fusion | flops 48351136 | bytes 401984 | tf_op jit(solution)/shard_map/while/body/eval_jaxpr/bqij,cbqj->cbi/dot_general | solution.py:43
  92.4 11.0 %broadcast_in_dim.105 = f32[16,3,4096]{1,2,0:T(8,128)} broadcast(f32[]{:T(128)} %constant.18.clone.1), dimensions={} | broadcast | bytes 786436 | tf_op jit(solution)/shard_map/broadcast_in_dim | solution.py:125
  103.5 2.2 scatter_fusion
  105.7 1.3 collective-permute-start.6
  107.0 4.5 collective-permute-start.7
  111.6 1.3 collective-permute-done.7
  112.9 0.1 fusion.112
  113.0 1.9 collective-permute-start.9
  115.0 7.5 %collective-permute-start.8 = (f32[3,6,10,1]{3,2,1,0:T(8,128)S(1)}, f32[3,6,10,1]{3,2,1,0:T(8,128)S(1)}, u32[]{:S(2)}, u32[]{:S(2)}) collective-permute-start(f32[3,6,10,1]{3,2,1,0:T(8,128)S(1)} %get-tuple-element.81), channel_id=1, source_target_pairs={{1,0},{2,1},{3,2},{4,3},{5,4},{6,5},{7,6},{9,8},{10,9},{11,10},{12... | collective-permute-start | bytes 2168 | tf_op jit(solution)/shard_map/ppermute | solution.py:26
  122.5 3.9 collective-permute-start.3
  126.5 1.9 collective-permute-start.2
  128.4 1.2 collective-permute-done.3
  129.6 6.6 %collective-permute-done.2 = f32[7,16,128]{2,0,1:T(8,128)S(1)} collective-permute-done((f32[7,16,128]{2,0,1:T(8,128)S(1)}, f32[7,16,128]{2,0,1:T(8,128)S(1)}, u32[]{:S(2)}, u32[]{:S(2)}) %collective-permute-start.2) | collective-permute-done | bytes 57376 | tf_op jit(solution)/shard_map/ppermute | solution.py:24
  136.3 0.6 gather_fusion.2
  137.2 321.7 %reduce-scatter.2.cloned.1.call-done = f32[1,3,4096]{1,2,0:T(8,128)} async-done(((f32[16,3,4096]{1,2,0:T(8,128)}), f32[1,3,4096]{1,2,0:T(8,128)}) %reduce-scatter.2.cloned.1.call-update) | async-done | bytes 49168 | tf_op jit(solution)/shard_map/reduce_scatter | solution.py:124
  458.9 2.2 copy.109
  461.1 0.1 fusion.106
  461.3 2.5 collective-permute-start.10
  463.8 1.9 collective-permute-start.11
  465.7 2.2 fusion.5
  468.0 0.8 collective-permute-done.11
  468.8 1.3 collective-permute-start.12
  470.1 4.5 collective-permute-start.13
  474.7 5.6 %fusion.57 = f32[3,16,128]{2,0,1:T(4,128)S(1)} fusion(f32[16,4,128]{2,1,0:T(4,128)S(1)} %bitcast.132, f32[16,128]{1,0:T(8,128)S(1)} %bitcast.150, f32[16,4,128]{2,1,0:T(4,128)S(1)} %bitcast.135, f32[16,128]{1,0:T(8,128)S(1)} %bitcast.153, f32[16,4,128]{2,1,0:T(4,128)S(1)} %bitcast.129, f32[16,128]{1,0:T(8,128)S(1)} %bitcast.147, ...), kind=kOutput, calls=%fused_computation.63 | convolution fusion | flops 48277504 | bytes 311296 | tf_op jit(solution)/shard_map/while/body/eval_jaxpr/bqij,cbqj->cbi/dot_general | solution.py:42
  480.3 0.1 fusion.111
  480.4 3.4 collective-permute-start.15
  483.9 6.0 %collective-permute-start.14 = (f32[3,6,10,1]{3,2,1,0:T(8,128)S(1)}, f32[3,6,10,1]{3,2,1,0:T(8,128)S(1)}, u32[]{:S(2)}, u32[]{:S(2)}) collective-permute-start(f32[3,6,10,1]{3,2,1,0:T(8,128)S(1)} %get-tuple-element.79), channel_id=1, source_target_pairs={{1,0},{2,1},{3,2},{4,3},{5,4},{6,5},{7,6},{9,8},{10,9},{11,10},{12... | collective-permute-start | bytes 2168 | tf_op jit(solution)/shard_map/ppermute | solution.py:26
  489.9 5.6 %multiply_add_fusion = (f32[3,16,128]{2,0,1:T(4,128)S(1)}, f32[3,16,128]{2,0,1:T(4,128)S(1)}) fusion(f32[3,16,128]{2,0,1:T(4,128)S(1)} %get-tuple-element.109, f32[16,128]{1,0:T(8,128)S(1)} %get-tuple-element.120, f32[3,16,128]{2,0,1:T(4,128)S(1)} %get-tuple-element.122, f32[3,16]{0,1:T(8,128)S(1)} %select_bitcast_fusion.1, f32[3,16,128]{2,0,1:T(4,128)S(1)} %fusion.57, ...), kind=kOutput, calls=%fused_computation.143 | convolution fusion | flops 48320512 | bytes 393408 | tf_op jit(solution)/shard_map/while/body/eval_jaxpr/bqij,cbqj->cbi/dot_general | solution.py:43
  495.5 0.6 copy.111
  496.2 0.6 copy.112
  496.8 0.8 fusion.80
  (61 shorter events, 1.1 us)
Async XLA Ops:
  7.2 451.7 %reduce-scatter.2.cloned.1.call-start = ((), (), s32[]{:S(2)}) async-start(), calls=%async_computation.1 | async-start | bytes 35651584 | tf_op jit(solution)/shard_map/reduce_scatter | solution.py:124
  9.5 68.0 %collective-permute-start.1 = (f32[7,16,128]{2,0,1:T(8,128)S(1)}, f32[7,16,128]{2,0,1:T(8,128)S(1)}, u32[]{:S(2)}, u32[]{:S(2)}) collective-permute-start(f32[7,16,128]{2,0,1:T(8,128)S(1)} %pad_maximum_fusion.5), channel_id=1, source_target_pairs={{1,0},{2,1},{3,2},{4,3},{5,4},{6,5},{7,6},{8,7},{9,8},{10,9},{11,1... | collective-permute-start | bytes 172040 | tf_op jit(solution)/shard_map/ppermute | solution.py:26
  16.3 61.3 %collective-permute-start = (f32[7,16,128]{2,0,1:T(8,128)S(1)}, f32[7,16,128]{2,0,1:T(8,128)S(1)}, u32[]{:S(2)}, u32[]{:S(2)}) collective-permute-start(f32[7,16,128]{2,0,1:T(8,128)S(1)} %pad_maximum_fusion.5), channel_id=1, source_target_pairs={{0,1},{1,2},{2,3},{3,4},{4,5},{5,6},{6,7},{7,8},{8,9},{9,10},{10,1... | collective-permute-start | bytes 172040 | tf_op jit(solution)/shard_map/ppermute | solution.py:24
  19.0 58.5 %collective-permute-start.5 = (f32[3,1,8,128]{3,2,1,0:T(8,128)S(1)}, f32[3,1,8,128]{3,2,1,0:T(8,128)S(1)}, u32[]{:S(2)}, u32[]{:S(2)}) collective-permute-start(f32[3,1,8,128]{3,2,1,0:T(8,128)S(1)} %get-tuple-element.108), channel_id=1, source_target_pairs={{0,32},{32,64},{64,96},{1,33},{33,65},{65,97},{2,34},{34,66},{66,9... | collective-permute-start | bytes 36872 | tf_op jit(solution)/shard_map/ppermute | solution.py:24
  20.9 56.6 %collective-permute-start.4 = (f32[3,1,8,128]{3,2,1,0:T(8,128)S(1)}, f32[3,1,8,128]{3,2,1,0:T(8,128)S(1)}, u32[]{:S(2)}, u32[]{:S(2)}) collective-permute-start(f32[3,1,8,128]{3,2,1,0:T(8,128)S(1)} %get-tuple-element.107), channel_id=1, source_target_pairs={{32,0},{64,32},{96,64},{33,1},{65,33},{97,65},{34,2},{66,34},{98,6... | collective-permute-start | bytes 36872 | tf_op jit(solution)/shard_map/ppermute | solution.py:26
  60.3 15.6 %copy-start.6 = (s32[16,1]{0,1:T(1,128)S(1)}, s32[16,1]{0,1:T(1,128)}, u32[]{:S(2)}) copy-start(s32[16,1]{0,1:T(1,128)} %param.15) | copy-start | bytes 196
  60.3 15.6 %copy-start.5 = (s32[16]{0:T(128)S(1)}, s32[16]{0:T(128)}, u32[]{:S(2)}) copy-start(s32[16]{0:T(128)} %param.16) | copy-start | bytes 196
  60.3 15.6 %copy-start.3 = (s32[16,3]{0,1:T(4,128)S(1)}, s32[16,3]{0,1:T(4,128)}, u32[]{:S(2)}) copy-start(s32[16,3]{0,1:T(4,128)} %param.13) | copy-start | bytes 580
  60.3 17.2 %copy-start.4 = (s32[16,3]{0,1:T(4,128)S(1)}, s32[16,3]{0,1:T(4,128)}, u32[]{:S(2)}) copy-start(s32[16,3]{0,1:T(4,128)} %param.14) | copy-start | bytes 580
  60.3 17.2 %copy-start = (f32[3,4,8,128]{3,2,1,0:T(8,128)S(1)}, f32[3,4,8,128]{3,2,1,0:T(8,128)}, u32[]{:S(2)}) copy-start(f32[3,4,8,128]{3,2,1,0:T(8,128)} %param.17) | copy-start | bytes 147460
  60.3 20.5 %copy-start.1 = (f32[3,16,128]{2,1,0:T(8,128)S(1)}, f32[3,16,128]{2,1,0:T(8,128)}, u32[]{:S(2)}) copy-start(f32[3,16,128]{2,1,0:T(8,128)} %param.9) | copy-start | bytes 73732
  80.8 5.6 %copy-start.2 = (f32[3,16,128]{2,1,0:T(8,128)S(1)}, f32[3,16,128]{2,1,0:T(8,128)}, u32[]{:S(2)}) copy-start(f32[3,16,128]{2,1,0:T(8,128)} %param.10) | copy-start | bytes 73732
  105.7 5.9 %collective-permute-start.6 = (f32[3,6,1,128]{3,2,1,0:T(1,128)S(1)}, f32[3,6,1,128]{3,2,1,0:T(1,128)S(1)}, u32[]{:S(2)}, u32[]{:S(2)}) collective-permute-start(f32[3,6,1,128]{3,2,1,0:T(1,128)S(1)} %get-tuple-element.104), channel_id=1, source_target_pairs={{8,0},{16,8},{24,16},{9,1},{17,9},{25,17},{10,2},{18,10},{26,18},{... | collective-permute-start | bytes 27656 | tf_op jit(solution)/shard_map/ppermute | solution.py:26
  107.0 5.9 %collective-permute-start.7 = (f32[3,6,1,128]{3,2,1,0:T(1,128)S(1)}, f32[3,6,1,128]{3,2,1,0:T(1,128)S(1)}, u32[]{:S(2)}, u32[]{:S(2)}) collective-permute-start(f32[3,6,1,128]{3,2,1,0:T(1,128)S(1)} %get-tuple-element.103), channel_id=1, source_target_pairs={{0,8},{8,16},{16,24},{1,9},{9,17},{17,25},{2,10},{10,18},{18,26},{... | collective-permute-start | bytes 27656 | tf_op jit(solution)/shard_map/ppermute | solution.py:24
  113.0 348.1 %collective-permute-start.9 = (f32[3,6,10,1]{3,2,1,0:T(8,128)S(1)}, f32[3,6,10,1]{3,2,1,0:T(8,128)S(1)}, u32[]{:S(2)}, u32[]{:S(2)}) collective-permute-start(f32[3,6,10,1]{3,2,1,0:T(8,128)S(1)} %get-tuple-element.82), channel_id=1, source_target_pairs={{0,1},{1,2},{2,3},{3,4},{4,5},{5,6},{6,7},{8,9},{9,10},{10,11},{11... | collective-permute-start | bytes 2168 | tf_op jit(solution)/shard_map/ppermute | solution.py:24
  115.0 346.2 %collective-permute-start.8 = (f32[3,6,10,1]{3,2,1,0:T(8,128)S(1)}, f32[3,6,10,1]{3,2,1,0:T(8,128)S(1)}, u32[]{:S(2)}, u32[]{:S(2)}) collective-permute-start(f32[3,6,10,1]{3,2,1,0:T(8,128)S(1)} %get-tuple-element.81), channel_id=1, source_target_pairs={{1,0},{2,1},{3,2},{4,3},{5,4},{6,5},{7,6},{9,8},{10,9},{11,10},{12... | collective-permute-start | bytes 2168 | tf_op jit(solution)/shard_map/ppermute | solution.py:26
  122.5 7.1 %collective-permute-start.3 = (f32[7,16,128]{2,0,1:T(8,128)S(1)}, f32[7,16,128]{2,0,1:T(8,128)S(1)}, u32[]{:S(2)}, u32[]{:S(2)}) collective-permute-start(f32[7,16,128]{2,0,1:T(8,128)S(1)} %pad_maximum_fusion.4), channel_id=1, source_target_pairs={{1,0},{2,1},{3,2},{4,3},{5,4},{6,5},{7,6},{8,7},{9,8},{10,9},{11,1... | collective-permute-start | bytes 172040 | tf_op jit(solution)/shard_map/ppermute | solution.py:26
  126.5 9.8 %collective-permute-start.2 = (f32[7,16,128]{2,0,1:T(8,128)S(1)}, f32[7,16,128]{2,0,1:T(8,128)S(1)}, u32[]{:S(2)}, u32[]{:S(2)}) collective-permute-start(f32[7,16,128]{2,0,1:T(8,128)S(1)} %pad_maximum_fusion.4), channel_id=1, source_target_pairs={{0,1},{1,2},{2,3},{3,4},{4,5},{5,6},{6,7},{7,8},{8,9},{9,10},{10,1... | collective-permute-start | bytes 172040 | tf_op jit(solution)/shard_map/ppermute | solution.py:24
  461.3 6.7 %collective-permute-start.10 = (f32[3,1,8,128]{3,2,1,0:T(8,128)S(1)}, f32[3,1,8,128]{3,2,1,0:T(8,128)S(1)}, u32[]{:S(2)}, u32[]{:S(2)}) collective-permute-start(f32[3,1,8,128]{3,2,1,0:T(8,128)S(1)} %get-tuple-element.106), channel_id=1, source_target_pairs={{32,0},{64,32},{96,64},{33,1},{65,33},{97,65},{34,2},{66,34},{98,6... | collective-permute-start | bytes 36872 | tf_op jit(solution)/shard_map/ppermute | solution.py:26
  463.8 5.0 collective-permute-start.11
  468.8 11.5 %collective-permute-start.12 = (f32[3,6,1,128]{3,2,1,0:T(1,128)S(1)}, f32[3,6,1,128]{3,2,1,0:T(1,128)S(1)}, u32[]{:S(2)}, u32[]{:S(2)}) collective-permute-start(f32[3,6,1,128]{3,2,1,0:T(1,128)S(1)} %get-tuple-element.102), channel_id=1, source_target_pairs={{8,0},{16,8},{24,16},{9,1},{17,9},{25,17},{10,2},{18,10},{26,18},{... | collective-permute-start | bytes 27656 | tf_op jit(solution)/shard_map/ppermute | solution.py:26
  470.1 10.2 %collective-permute-start.13 = (f32[3,6,1,128]{3,2,1,0:T(1,128)S(1)}, f32[3,6,1,128]{3,2,1,0:T(1,128)S(1)}, u32[]{:S(2)}, u32[]{:S(2)}) collective-permute-start(f32[3,6,1,128]{3,2,1,0:T(1,128)S(1)} %get-tuple-element.101), channel_id=1, source_target_pairs={{0,8},{8,16},{16,24},{1,9},{9,17},{17,25},{2,10},{10,18},{18,26},{... | collective-permute-start | bytes 27656 | tf_op jit(solution)/shard_map/ppermute | solution.py:24
  480.4 16.3 %collective-permute-start.15 = (f32[3,6,10,1]{3,2,1,0:T(8,128)S(1)}, f32[3,6,10,1]{3,2,1,0:T(8,128)S(1)}, u32[]{:S(2)}, u32[]{:S(2)}) collective-permute-start(f32[3,6,10,1]{3,2,1,0:T(8,128)S(1)} %get-tuple-element.80), channel_id=1, source_target_pairs={{0,1},{1,2},{2,3},{3,4},{4,5},{5,6},{6,7},{8,9},{9,10},{10,11},{11... | collective-permute-start | bytes 2168 | tf_op jit(solution)/shard_map/ppermute | solution.py:24
  483.9 12.9 %collective-permute-start.14 = (f32[3,6,10,1]{3,2,1,0:T(8,128)S(1)}, f32[3,6,10,1]{3,2,1,0:T(8,128)S(1)}, u32[]{:S(2)}, u32[]{:S(2)}) collective-permute-start(f32[3,6,10,1]{3,2,1,0:T(8,128)S(1)} %get-tuple-element.79), channel_id=1, source_target_pairs={{1,0},{2,1},{3,2},{4,3},{5,4},{6,5},{7,6},{9,8},{10,9},{11,10},{12... | collective-permute-start | bytes 2168 | tf_op jit(solution)/shard_map/ppermute | solution.py:26
Sparse Core Ops, SparseCore 0:
  105.8 353.0 reduce-scatter.1
where the time goes:
time: 505 us; the launch traced here: 504 us
  waiting for transfers between devices  332 us (66%)
  starting transfers between devices  55.1 us (11%)
  local copies, waits for them, and re-layouts  37 us (7%)
  blocking collectives  34.2 us (7%)
  matrix products  22.8 us (5%)
  between operations  14.5 us (3%)
  other arithmetic  9.07 us (2%)
    reduce_scatter x1, waiting for transfers between devices, local(): lax.psum_scatter(jnp.zeros((1 * lax.axis_size(('gx', 'gy')), 3, cell_coun...  322 us
    all_gather x1, blocking collectives, local(): lax.all_gather(flat_fluid[None], ('gx', 'gy'), axis=0, tiled=True)  34.2 us
    ppermute x8, starting transfers between devices, padded_2(): lax.ppermute(head, axis, [((i + 1) % count, i) for i in range(ends)])  33 us
    ppermute x8, starting transfers between devices, padded_2(): lax.ppermute(tail, axis, [(i, (i + 1) % count) for i in range(ends)])  22.1 us
    all_gather x1, local copies, waits for them, and re-layouts, local(): lax.all_gather(flat_fluid[None], ('gx', 'gy'), axis=0, tiled=True)  15.6 us
    dot_general x2, matrix products, contact(): pull_vel = jnp.einsum('bqij,cbqj->cbi', kernel, near_vel, precision=highest)  11.6 us
    dot_general x2, matrix products, contact(): pull_pos = jnp.einsum('bqij,cbqj->cbi', kernel, near_pos, precision=highest)  11.2 us
    broadcast_in_dim x1, local copies, waits for them, and re-layouts, local(): jnp.zeros((1 * lax.axis_size(('gx', 'gy')), 3, cell_count), jnp.float32)  11 us
  transfers between devices with their start and end apart: 17, of which 5 were waited for; matrix products, arithmetic and copies ran while one was open for 7% of the time, Pallas kernels for 0%

commit v1 on v0

--- a/solution.py
+++ b/solution.py
@@ -89,7 +89,12 @@
     ).astype(jnp.float32)
     carried = weights * occupied
     target = bin_box[:, 0]
-    box_piece = lax.all_gather(flat_fluid[None], ("gx", "gy"), axis=0, tiled=True)
+    box_piece = jnp.concatenate(
+        lax.all_to_all(
+            jnp.stack([flat_fluid[None]] * lax.axis_size(("gx", "gy"))), ("gx", "gy"), 0, 0
+        ),
+        axis=0,
+    )
     first_box = jnp.int32(0)
     local_box = jnp.clip(target, 0, box_piece.shape[0] - 1)
     inside = (target >= first_box) & (target < first_box + box_piece.shape[0])

time: 505 us -> 484 us (0.958)
  blocking collectives: 34.2 us -> 0 us
  starting transfers between devices: 55.1 us -> 61.1 us
    all_gather x1 -> x0, blocking collectives: 34.2 us -> none  [local(): lax.all_gather(flat_fluid[None], ('gx', 'gy'), axis=0, tiled=True)]
    all_to_all x0 -> x1, local copies, waits for them, and re-layouts: none -> 16.1 us  [local(): lax.all_to_all(jnp.stack([flat_fluid[None]] * lax.axis_size(('gx', 'gy'))...]
    all_gather x1 -> x0, local copies, waits for them, and re-layouts: 15.6 us -> none  [local(): lax.all_gather(flat_fluid[None], ('gx', 'gy'), axis=0, tiled=True)]
    all_to_all x0 -> x1, starting transfers between devices: none -> 5.95 us  [local(): lax.all_to_all(jnp.stack([flat_fluid[None]] * lax.axis_size(('gx', 'gy'))...]
  transfers between devices with their start and end apart: 17 -> 18, of which waited for: 5 -> 6; matrix products, arithmetic and copies ran while one was open for 7% -> 7% of each run, Pallas kernels for 0% -> 0%
where the time goes in v1:
time: 484 us; the launch traced here: 482 us
  waiting for transfers between devices  333 us (69%)
  starting transfers between devices  61.1 us (13%)
  local copies, waits for them, and re-layouts  39.2 us (8%)
  matrix products  22.8 us (5%)
  between operations  14.5 us (3%)
  other arithmetic  11.8 us (2%)
    reduce_scatter x1, waiting for transfers between devices, local(): lax.psum_scatter(jnp.zeros((1 * lax.axis_size(('gx', 'gy')), 3, cell_coun...  322 us
    ppermute x8, starting transfers between devices, padded_2(): lax.ppermute(head, axis, [((i + 1) % count, i) for i in range(ends)])  32.8 us
    ppermute x8, starting transfers between devices, padded_2(): lax.ppermute(tail, axis, [(i, (i + 1) % count) for i in range(ends)])  22.3 us
    all_to_all x1, local copies, waits for them, and re-layouts, local(): lax.all_to_all(jnp.stack([flat_fluid[None]] * lax.axis_size(('gx', 'gy'))...  16.1 us
    dot_general x2, matrix products, contact(): pull_vel = jnp.einsum('bqij,cbqj->cbi', kernel, near_vel, precision=highest)  11.6 us
    dot_general x2, matrix products, contact(): pull_pos = jnp.einsum('bqij,cbqj->cbi', kernel, near_pos, precision=highest)  11.2 us
    broadcast_in_dim x1, local copies, waits for them, and re-layouts, local(): jnp.zeros((1 * lax.axis_size(('gx', 'gy')), 3, cell_count), jnp.float32)  11 us
    ppermute x8, waiting for transfers between devices, padded_2(): lax.ppermute(tail, axis, [(i, (i + 1) % count) for i in range(ends)])  10.2 us
  transfers between devices with their start and end apart: 18, of which 6 were waited for; matrix products, arithmetic and copies ran while one was open for 7% of the time, Pallas kernels for 0%

profile of v1, /device:TPU:6, one launch (start us, length us, event | category | flops | bytes accessed | tf_op | source)
XLA Modules:
  0.0 482.4 jit_solution(9920169327509049612)
XLA Ops:
  7.2 0.8 fusion.94
  8.0 0.8 copy_bitcast_fusion.1
  8.8 6.8 %collective-permute-start.1 = (f32[7,16,128]{2,0,1:T(8,128)S(1)}, f32[7,16,128]{2,0,1:T(8,128)S(1)}, u32[]{:S(2)}, u32[]{:S(2)}) collective-permute-start(f32[7,16,128]{2,0,1:T(8,128)S(1)} %pad_maximum_fusion.5), channel_id=1, source_target_pairs={{1,0},{2,1},{3,2},{4,3},{5,4},{6,5},{7,6},{8,7},{9,8},{10,9},{11,1... | collective-permute-start | bytes 172040 | tf_op jit(solution)/shard_map/ppermute | solution.py:26
  15.6 1.9 collective-permute-start
  17.5 0.8 copy.108
  18.4 1.6 stack.3
  20.0 5.9 %all-to-all-start = ((f32[16,1,3,4096]{3,1,2,0:T(1,128)}), f32[16,1,3,4096]{3,1,2,0:T(1,128)S(1)}, u32[]{:S(2)}, u32[]{:S(2)}) async-start(f32[16,1,3,4096]{3,1,2,0:T(1,128)} %stack.3), calls=%async_computation | async-start | bytes 1572864 | tf_op jit(solution)/shard_map/all_to_all | solution.py:93
  26.0 0.7 fusion.115
  26.7 2.0 collective-permute-start.5
  28.8 3.5 collective-permute-start.4
  32.3 0.7 slice_bitcast_fusion.2
  33.0 0.7 and_bitcast_fusion
  33.7 0.7 fusion.97
  34.4 0.7 compare_select_fusion
  35.2 0.7 convert_element_type.5
  36.0 0.8 constant_dynamic-update-slice_fusion.1
  36.9 0.6 gather_fusion
  37.8 2.2 fusion.2
  40.1 5.6 %fusion.49 = f32[3,16,128]{2,0,1:T(4,128)S(1)} fusion(f32[16,4,128]{2,1,0:T(4,128)S(1)} %bitcast.143, f32[16,128]{1,0:T(8,128)S(1)} %get-tuple-element.114, f32[16,4,128]{2,1,0:T(4,128)S(1)} %bitcast.146, f32[16,128]{1,0:T(8,128)S(1)} %get-tuple-element.113, f32[16,4,128]{2,1,0:T(4,128)S(1)} %bitcast.140, f32[16,128]{1,0:T(8,128)S(1)} %get-tuple-element.112, ...), kind=kOutput, calls=%fused_computation.55 | convolution fusion | flops 48277504 | bytes 311296 | tf_op jit(solution)/shard_map/while/body/eval_jaxpr/bqij,cbqj->cbi/dot_general | solution.py:42
  45.7 16.1 %copy.80 = f32[16,1,3,4096]{2,3,0,1:T(8,128)} copy(f32[16,1,3,4096]{3,1,2,0:T(1,128)S(1)} %all-to-all-done) | data formatting | bytes 1572864 | tf_op jit(solution)/shard_map/all_to_all | solution.py:93
  61.8 1.3 gather_fusion.1
  63.1 5.9 %multiply_reduce_fusion = (f32[3,16]{0,1:T(8,128)S(1)}, f32[3,16]{0,1:T(8,128)S(1)}, f32[3,16,128]{2,0,1:T(4,128)S(1)}, f32[3,16,128]{2,0,1:T(4,128)S(1)}) fusion(f32[16,128]{1,0:T(8,128)S(1)} %get-tuple-element.118, f32[3,16]{0,1:T(8,128)S(1)} %select_bitcast_fusion.1, f32[3,16,128]{2,1,0:T(8,128)S(1)} %copy-done.2, ...), kind=kOutput, calls=%fused_computation.142 | convolution fusion | flops 48351136 | bytes 401984 | tf_op jit(solution)/shard_map/while/body/eval_jaxpr/bqij,cbqj->cbi/dot_general | solution.py:43
  69.1 11.0 %broadcast_in_dim.105 = f32[16,3,4096]{1,2,0:T(8,128)} broadcast(f32[]{:T(128)} %constant.18.clone.1), dimensions={} | broadcast | bytes 786436 | tf_op jit(solution)/shard_map/broadcast_in_dim | solution.py:130
  80.2 2.2 scatter_fusion
  82.4 1.3 collective-permute-start.6
  83.7 4.5 collective-permute-start.7
  88.3 1.3 collective-permute-done.7
  89.7 1.9 collective-permute-start.9
  91.7 7.5 %collective-permute-start.8 = (f32[3,6,10,1]{3,2,1,0:T(8,128)S(1)}, f32[3,6,10,1]{3,2,1,0:T(8,128)S(1)}, u32[]{:S(2)}, u32[]{:S(2)}) collective-permute-start(f32[3,6,10,1]{3,2,1,0:T(8,128)S(1)} %get-tuple-element.78), channel_id=1, source_target_pairs={{1,0},{2,1},{3,2},{4,3},{5,4},{6,5},{7,6},{9,8},{10,9},{11,10},{12... | collective-permute-start | bytes 2168 | tf_op jit(solution)/shard_map/ppermute | solution.py:26
  99.3 3.9 collective-permute-start.3
  103.1 2.0 collective-permute-start.2
  105.6 8.0 %collective-permute-done.2 = f32[7,16,128]{2,0,1:T(8,128)S(1)} collective-permute-done((f32[7,16,128]{2,0,1:T(8,128)S(1)}, f32[7,16,128]{2,0,1:T(8,128)S(1)}, u32[]{:S(2)}, u32[]{:S(2)}) %collective-permute-start.2) | collective-permute-done | bytes 57376 | tf_op jit(solution)/shard_map/ppermute | solution.py:24
  113.6 0.6 gather_fusion.2
  114.5 322.4 %reduce-scatter.2.cloned.1.call-done = f32[1,3,4096]{1,2,0:T(8,128)} async-done(((f32[16,3,4096]{1,2,0:T(8,128)}), f32[1,3,4096]{1,2,0:T(8,128)}) %reduce-scatter.2.cloned.1.call-update) | async-done | bytes 49168 | tf_op jit(solution)/shard_map/reduce_scatter | solution.py:129
  436.9 2.2 copy.88
  439.3 2.5 collective-permute-start.10
  441.8 1.9 collective-permute-start.11
  443.8 2.3 fusion.5
  446.0 0.8 collective-permute-done.11
  446.9 1.3 collective-permute-start.12
  448.2 4.5 collective-permute-start.13
  452.7 5.6 %fusion.57 = f32[3,16,128]{2,0,1:T(4,128)S(1)} fusion(f32[16,4,128]{2,1,0:T(4,128)S(1)} %bitcast.134, f32[16,128]{1,0:T(8,128)S(1)} %bitcast.152, f32[16,4,128]{2,1,0:T(4,128)S(1)} %bitcast.137, f32[16,128]{1,0:T(8,128)S(1)} %bitcast.155, f32[16,4,128]{2,1,0:T(4,128)S(1)} %bitcast.131, f32[16,128]{1,0:T(8,128)S(1)} %bitcast.149, ...), kind=kOutput, calls=%fused_computation.63 | convolution fusion | flops 48277504 | bytes 311296 | tf_op jit(solution)/shard_map/while/body/eval_jaxpr/bqij,cbqj->cbi/dot_general | solution.py:42
  458.5 3.4 collective-permute-start.15
  461.9 6.0 %collective-permute-start.14 = (f32[3,6,10,1]{3,2,1,0:T(8,128)S(1)}, f32[3,6,10,1]{3,2,1,0:T(8,128)S(1)}, u32[]{:S(2)}, u32[]{:S(2)}) collective-permute-start(f32[3,6,10,1]{3,2,1,0:T(8,128)S(1)} %get-tuple-element.76), channel_id=1, source_target_pairs={{1,0},{2,1},{3,2},{4,3},{5,4},{6,5},{7,6},{9,8},{10,9},{11,10},{12... | collective-permute-start | bytes 2168 | tf_op jit(solution)/shard_map/ppermute | solution.py:26
  467.9 5.6 %multiply_add_fusion = (f32[3,16,128]{2,0,1:T(4,128)S(1)}, f32[3,16,128]{2,0,1:T(4,128)S(1)}) fusion(f32[3,16,128]{2,0,1:T(4,128)S(1)} %get-tuple-element.106, f32[16,128]{1,0:T(8,128)S(1)} %get-tuple-element.117, f32[3,16,128]{2,0,1:T(4,128)S(1)} %get-tuple-element.119, f32[3,16]{0,1:T(8,128)S(1)} %select_bitcast_fusion.1, f32[3,16,128]{2,0,1:T(4,128)S(1)} %fusion.57, ...), kind=kOutput, calls=%fused_computation.144 | convolution fusion | flops 48320512 | bytes 393408 | tf_op jit(solution)/shard_map/while/body/eval_jaxpr/bqij,cbqj->cbi/dot_general | solution.py:43
  473.6 0.6 copy.90
  474.2 0.6 copy.91
  474.8 0.8 fusion.80
  (54 shorter events, 2.1 us)
Async XLA Ops:
  7.2 32.9 %copy-start.1 = (f32[3,16,128]{2,1,0:T(8,128)S(1)}, f32[3,16,128]{2,1,0:T(8,128)}, u32[]{:S(2)}) copy-start(f32[3,16,128]{2,1,0:T(8,128)} %param.9) | copy-start | bytes 73732
  8.8 28.1 %collective-permute-start.1 = (f32[7,16,128]{2,0,1:T(8,128)S(1)}, f32[7,16,128]{2,0,1:T(8,128)S(1)}, u32[]{:S(2)}, u32[]{:S(2)}) collective-permute-start(f32[7,16,128]{2,0,1:T(8,128)S(1)} %pad_maximum_fusion.5), channel_id=1, source_target_pairs={{1,0},{2,1},{3,2},{4,3},{5,4},{6,5},{7,6},{8,7},{9,8},{10,9},{11,1... | collective-permute-start | bytes 172040 | tf_op jit(solution)/shard_map/ppermute | solution.py:26
  15.6 21.3 %collective-permute-start = (f32[7,16,128]{2,0,1:T(8,128)S(1)}, f32[7,16,128]{2,0,1:T(8,128)S(1)}, u32[]{:S(2)}, u32[]{:S(2)}) collective-permute-start(f32[7,16,128]{2,0,1:T(8,128)S(1)} %pad_maximum_fusion.5), channel_id=1, source_target_pairs={{0,1},{1,2},{2,3},{3,4},{4,5},{5,6},{6,7},{7,8},{8,9},{9,10},{10,1... | collective-permute-start | bytes 172040 | tf_op jit(solution)/shard_map/ppermute | solution.py:24
  20.0 25.7 %all-to-all-start = ((f32[16,1,3,4096]{3,1,2,0:T(1,128)}), f32[16,1,3,4096]{3,1,2,0:T(1,128)S(1)}, u32[]{:S(2)}, u32[]{:S(2)}) async-start(f32[16,1,3,4096]{3,1,2,0:T(1,128)} %stack.3), calls=%async_computation | async-start | bytes 1572864 | tf_op jit(solution)/shard_map/all_to_all | solution.py:93
  25.9 411.0 %reduce-scatter.2.cloned.1.call-start = ((), (), s32[]{:S(2)}) async-start(), calls=%async_computation.2 | async-start | bytes 35651584 | tf_op jit(solution)/shard_map/reduce_scatter | solution.py:129
  26.7 9.3 %collective-permute-start.5 = (f32[3,1,8,128]{3,2,1,0:T(8,128)S(1)}, f32[3,1,8,128]{3,2,1,0:T(8,128)S(1)}, u32[]{:S(2)}, u32[]{:S(2)}) collective-permute-start(f32[3,1,8,128]{3,2,1,0:T(8,128)S(1)} %get-tuple-element.105), channel_id=1, source_target_pairs={{0,32},{32,64},{64,96},{1,33},{33,65},{65,97},{2,34},{34,66},{66,9... | collective-permute-start | bytes 36872 | tf_op jit(solution)/shard_map/ppermute | solution.py:24
  28.8 8.1 %collective-permute-start.4 = (f32[3,1,8,128]{3,2,1,0:T(8,128)S(1)}, f32[3,1,8,128]{3,2,1,0:T(8,128)S(1)}, u32[]{:S(2)}, u32[]{:S(2)}) collective-permute-start(f32[3,1,8,128]{3,2,1,0:T(8,128)S(1)} %get-tuple-element.104), channel_id=1, source_target_pairs={{32,0},{64,32},{96,64},{33,1},{65,33},{97,65},{34,2},{66,34},{98,6... | collective-permute-start | bytes 36872 | tf_op jit(solution)/shard_map/ppermute | solution.py:26
  45.7 17.4 %copy-start.2 = (f32[3,16,128]{2,1,0:T(8,128)S(1)}, f32[3,16,128]{2,1,0:T(8,128)}, u32[]{:S(2)}) copy-start(f32[3,16,128]{2,1,0:T(8,128)} %param.10) | copy-start | bytes 73732
  82.4 356.8 %copy-start = (f32[3,4,8,128]{3,2,1,0:T(8,128)S(1)}, f32[3,4,8,128]{3,2,1,0:T(8,128)}, u32[]{:S(2)}) copy-start(f32[3,4,8,128]{3,2,1,0:T(8,128)} %param.17) | copy-start | bytes 147460
  82.4 5.9 %collective-permute-start.6 = (f32[3,6,1,128]{3,2,1,0:T(1,128)S(1)}, f32[3,6,1,128]{3,2,1,0:T(1,128)S(1)}, u32[]{:S(2)}, u32[]{:S(2)}) collective-permute-start(f32[3,6,1,128]{3,2,1,0:T(1,128)S(1)} %get-tuple-element.101), channel_id=1, source_target_pairs={{8,0},{16,8},{24,16},{9,1},{17,9},{25,17},{10,2},{18,10},{26,18},{... | collective-permute-start | bytes 27656 | tf_op jit(solution)/shard_map/ppermute | solution.py:26
  83.7 5.9 %collective-permute-start.7 = (f32[3,6,1,128]{3,2,1,0:T(1,128)S(1)}, f32[3,6,1,128]{3,2,1,0:T(1,128)S(1)}, u32[]{:S(2)}, u32[]{:S(2)}) collective-permute-start(f32[3,6,1,128]{3,2,1,0:T(1,128)S(1)} %get-tuple-element.100), channel_id=1, source_target_pairs={{0,8},{8,16},{16,24},{1,9},{9,17},{17,25},{2,10},{10,18},{18,26},{... | collective-permute-start | bytes 27656 | tf_op jit(solution)/shard_map/ppermute | solution.py:24
  89.7 349.4 %collective-permute-start.9 = (f32[3,6,10,1]{3,2,1,0:T(8,128)S(1)}, f32[3,6,10,1]{3,2,1,0:T(8,128)S(1)}, u32[]{:S(2)}, u32[]{:S(2)}) collective-permute-start(f32[3,6,10,1]{3,2,1,0:T(8,128)S(1)} %get-tuple-element.79), channel_id=1, source_target_pairs={{0,1},{1,2},{2,3},{3,4},{4,5},{5,6},{6,7},{8,9},{9,10},{10,11},{11... | collective-permute-start | bytes 2168 | tf_op jit(solution)/shard_map/ppermute | solution.py:24
  91.7 347.5 %collective-permute-start.8 = (f32[3,6,10,1]{3,2,1,0:T(8,128)S(1)}, f32[3,6,10,1]{3,2,1,0:T(8,128)S(1)}, u32[]{:S(2)}, u32[]{:S(2)}) collective-permute-start(f32[3,6,10,1]{3,2,1,0:T(8,128)S(1)} %get-tuple-element.78), channel_id=1, source_target_pairs={{1,0},{2,1},{3,2},{4,3},{5,4},{6,5},{7,6},{9,8},{10,9},{11,10},{12... | collective-permute-start | bytes 2168 | tf_op jit(solution)/shard_map/ppermute | solution.py:26
  99.3 6.4 %collective-permute-start.3 = (f32[7,16,128]{2,0,1:T(8,128)S(1)}, f32[7,16,128]{2,0,1:T(8,128)S(1)}, u32[]{:S(2)}, u32[]{:S(2)}) collective-permute-start(f32[7,16,128]{2,0,1:T(8,128)S(1)} %pad_maximum_fusion.4), channel_id=1, source_target_pairs={{1,0},{2,1},{3,2},{4,3},{5,4},{6,5},{7,6},{8,7},{9,8},{10,9},{11,1... | collective-permute-start | bytes 172040 | tf_op jit(solution)/shard_map/ppermute | solution.py:26
  103.1 10.4 %collective-permute-start.2 = (f32[7,16,128]{2,0,1:T(8,128)S(1)}, f32[7,16,128]{2,0,1:T(8,128)S(1)}, u32[]{:S(2)}, u32[]{:S(2)}) collective-permute-start(f32[7,16,128]{2,0,1:T(8,128)S(1)} %pad_maximum_fusion.4), channel_id=1, source_target_pairs={{0,1},{1,2},{2,3},{3,4},{4,5},{5,6},{6,7},{7,8},{8,9},{9,10},{10,1... | collective-permute-start | bytes 172040 | tf_op jit(solution)/shard_map/ppermute | solution.py:24
  439.3 6.7 %collective-permute-start.10 = (f32[3,1,8,128]{3,2,1,0:T(8,128)S(1)}, f32[3,1,8,128]{3,2,1,0:T(8,128)S(1)}, u32[]{:S(2)}, u32[]{:S(2)}) collective-permute-start(f32[3,1,8,128]{3,2,1,0:T(8,128)S(1)} %get-tuple-element.103), channel_id=1, source_target_pairs={{32,0},{64,32},{96,64},{33,1},{65,33},{97,65},{34,2},{66,34},{98,6... | collective-permute-start | bytes 36872 | tf_op jit(solution)/shard_map/ppermute | solution.py:26
  441.8 5.0 %collective-permute-start.11 = (f32[3,1,8,128]{3,2,1,0:T(8,128)S(1)}, f32[3,1,8,128]{3,2,1,0:T(8,128)S(1)}, u32[]{:S(2)}, u32[]{:S(2)}) collective-permute-start(f32[3,1,8,128]{3,2,1,0:T(8,128)S(1)} %get-tuple-element.102), channel_id=1, source_target_pairs={{0,32},{32,64},{64,96},{1,33},{33,65},{65,97},{2,34},{34,66},{66,9... | collective-permute-start | bytes 36872 | tf_op jit(solution)/shard_map/ppermute | solution.py:24
  446.9 11.5 %collective-permute-start.12 = (f32[3,6,1,128]{3,2,1,0:T(1,128)S(1)}, f32[3,6,1,128]{3,2,1,0:T(1,128)S(1)}, u32[]{:S(2)}, u32[]{:S(2)}) collective-permute-start(f32[3,6,1,128]{3,2,1,0:T(1,128)S(1)} %get-tuple-element.99), channel_id=1, source_target_pairs={{8,0},{16,8},{24,16},{9,1},{17,9},{25,17},{10,2},{18,10},{26,18},{... | collective-permute-start | bytes 27656 | tf_op jit(solution)/shard_map/ppermute | solution.py:26
  448.2 10.2 %collective-permute-start.13 = (f32[3,6,1,128]{3,2,1,0:T(1,128)S(1)}, f32[3,6,1,128]{3,2,1,0:T(1,128)S(1)}, u32[]{:S(2)}, u32[]{:S(2)}) collective-permute-start(f32[3,6,1,128]{3,2,1,0:T(1,128)S(1)} %get-tuple-element.98), channel_id=1, source_target_pairs={{0,8},{8,16},{16,24},{1,9},{9,17},{17,25},{2,10},{10,18},{18,26},{... | collective-permute-start | bytes 27656 | tf_op jit(solution)/shard_map/ppermute | solution.py:24
  458.5 16.3 %collective-permute-start.15 = (f32[3,6,10,1]{3,2,1,0:T(8,128)S(1)}, f32[3,6,10,1]{3,2,1,0:T(8,128)S(1)}, u32[]{:S(2)}, u32[]{:S(2)}) collective-permute-start(f32[3,6,10,1]{3,2,1,0:T(8,128)S(1)} %get-tuple-element.77), channel_id=1, source_target_pairs={{0,1},{1,2},{2,3},{3,4},{4,5},{5,6},{6,7},{8,9},{9,10},{10,11},{11... | collective-permute-start | bytes 2168 | tf_op jit(solution)/shard_map/ppermute | solution.py:24
  461.9 12.9 %collective-permute-start.14 = (f32[3,6,10,1]{3,2,1,0:T(8,128)S(1)}, f32[3,6,10,1]{3,2,1,0:T(8,128)S(1)}, u32[]{:S(2)}, u32[]{:S(2)}) collective-permute-start(f32[3,6,10,1]{3,2,1,0:T(8,128)S(1)} %get-tuple-element.76), channel_id=1, source_target_pairs={{1,0},{2,1},{3,2},{4,3},{5,4},{6,5},{7,6},{9,8},{10,9},{11,10},{12... | collective-permute-start | bytes 2168 | tf_op jit(solution)/shard_map/ppermute | solution.py:26
Sparse Core Ops, SparseCore 0:
  82.5 354.3 reduce-scatter.1
